TPU v7x, 128 devices: a whole 4x4x4 slice. The times are simulated.
128 devices in a mesh: dp: 16 (over x, y_lo, core), tensor: 8 (over z, y_hi).
Axes of the slice: x: 4, y: 4 (y_hi: 2, y_lo: 2; y = y_hi * 2 + y_lo), z: 4, core: 2. Of those that a mesh axis runs over, the one named last changes fastest.
Arguments:
- acts: bfloat16 [128, 64, 4096], P('dp'), may hold values from -6 to 6
- output_gradient: bfloat16 [128, 64, 4096], P('dp', None, 'tensor'), may hold values from -6 to 6
- adapter_down_matrix: bfloat16 [64, 4096], replicated, may hold values from -0.09375 to 0.09375
- adapter_up_matrix: bfloat16 [4096, 64], P('tensor'), may hold values from -0.09375 to 0.09375
- counts: int32 [128], P('dp'), may hold values from 8 to 64, as said below
- signs: int32 [8, 512, 128, 1024], P('tensor', 'dp'), may hold values from 0 to 255
- bank: bfloat16 [128, 8192], replicated, may hold values from -6 to 6
- validation_rows: int32 [64], replicated, may hold values from 0 to 127
Outputs:
- features: float32 [128, 8192], P(('dp', 'tensor'))
- scores: float32 [128, 64], P(('dp', 'tensor'))
Inputs may be any that keep to these rules, and one draw needn't show every extreme that they name: Tokens at positions below counts are real; at least one example has all 64 tokens real. Each word carries 8 independent signs in its low 8 bits.
All inputs are finite; a program needn't handle non-finite values.
Results may differ from a plain program's by a relative error of at most 0.0042.
Values may be sent and summed in bfloat16 or wider, within the bound.
A program may use at most 128 MiB of HBM per device.

v0:
```python
import math

import jax
import jax.numpy as jnp
from jax import lax
from jax.sharding import PartitionSpec as P


def per_device(
    acts,
    output_gradient,
    adapter_down_matrix,
    adapter_up_matrix,
    counts,
    signs,
    bank,
    validation_rows,
):
    seq_len = acts.shape[1]
    slice_width = output_gradient.shape[2]
    offset = lax.axis_index("tensor") * slice_width
    positions = jnp.arange(seq_len, dtype=jnp.int32)
    keep_mask = positions[None, :] < counts[:, None]
    masked_output = jnp.where(
        keep_mask[:, :, None], output_gradient, jnp.zeros_like(output_gradient)
    )
    hidden_state = lax.dot_general(
        acts, adapter_down_matrix, (((2,), (1,)), ((), ())), preferred_element_type=jnp.float32
    ).astype(jnp.bfloat16)
    partial_u = lax.dot_general(
        masked_output,
        adapter_up_matrix,
        (((2,), (0,)), ((), ())),
        preferred_element_type=jnp.float32,
    )
    coupled_gradient = lax.psum(partial_u, "tensor").astype(jnp.bfloat16)
    local_acts = lax.dynamic_slice_in_dim(acts, offset, slice_width, 2)
    grad_a = jnp.einsum(
        "esj,esr->jer", local_acts, coupled_gradient, preferred_element_type=jnp.float32
    )
    grad_b = jnp.einsum(
        "esj,esr->jer", masked_output, hidden_state, preferred_element_type=jnp.float32
    )
    gradient = jnp.concatenate([grad_a, grad_b], axis=2).astype(jnp.bfloat16)
    moved = lax.all_to_all(gradient, "dp", split_axis=0, concat_axis=1, tiled=True)
    sign_words = signs.reshape(signs.shape[1], signs.shape[2], signs.shape[3])
    proj_len = 8 * sign_words.shape[2]
    column_blocks = []
    for bit_number in range(8):
        bit_vals = jnp.bitwise_and(jnp.right_shift(sign_words, bit_number), 1)
        sign_block = (2 * bit_vals - 1).astype(jnp.bfloat16)
        column_blocks.append(
            lax.dot_general(
                moved, sign_block, (((0, 2), (0, 1)), ((), ())), preferred_element_type=jnp.float32
            )
        )
    projected = jnp.concatenate(column_blocks, axis=1)
    summed = lax.psum_scatter(projected, ("dp", "tensor"), scatter_dimension=0, tiled=True)
    mean_sq = jnp.mean(summed * summed, axis=1, keepdims=True)
    features = summed * lax.rsqrt(mean_sq + 1e-06)
    one_hot = (
        validation_rows[:, None] == jnp.arange(bank.shape[0], dtype=jnp.int32)[None, :]
    ).astype(jnp.bfloat16)
    chosen = jnp.dot(one_hot, bank, preferred_element_type=jnp.float32)
    scores = lax.dot_general(
        features, chosen, (((1,), (1,)), ((), ())), precision=lax.Precision.HIGHEST
    ) / math.sqrt(proj_len)
    return (features, scores)


def solution(mesh):
    in_specs = (
        P("dp", None, None),
        P("dp", None, "tensor"),
        P(),
        P("tensor", None),
        P("dp"),
        P("tensor", "dp", None, None),
        P(),
        P(),
    )
    out_specs = (P(("dp", "tensor"), None), P(("dp", "tensor"), None))
    return jax.shard_map(
        per_device, mesh=mesh, in_specs=in_specs, out_specs=out_specs, check_vma=False
    )
```

profile of v0, /device:TPU:0, one launch (start us, length us, event | category | flops | bytes accessed | tf_op | source)
XLA Modules:
  0.0 296.0 jit_solution(13285525171722058543)
XLA Ops:
  7.2 0.0 copy-start
  7.2 0.0 all-reduce.4.cloned.1.call-start
  7.2 0.9 iota_compare_fusion.2
  8.1 1.4 fusion.87
  9.5 48.1 %all-reduce.5 = bf16[8,64,64]{2,1,0:T(8,128)(2,1)S(1)} all-reduce(f32[8,64,64]{2,1,0:T(8,128)S(1)} %fusion.87), channel_id=1, replica_groups=mesh['dp'=16,'tensor'=8] {'tensor'}, use_global_device_ids=true, to_apply=%region_0.1 | all-reduce | flops 32768 | bytes 196608 | tf_op jit(solution)/shard_map/psum | solution.py:36
  57.6 4.9 %fusion.73 = bf16[512,8,64]{0,2,1:T(8,128)(2,1)} fusion(bf16[8,64,4096]{2,1,0:T(8,128)(2,1)} %param.8, bf16[64,4096]{1,0:T(8,128)(2,1)} %param.10, bf16[8,64,512]{2,1,0:T(8,128)(2,1)} %param.9, pred[8,64]{1,0:T(8,128)(4,1)S(1)} %iota_compare_fusion.2), kind=kOutput, calls=%fused_computation.43 | convolution fusion | flops 302546944 | bytes 5767680 | tf_op jit(solution)/shard_map/esj,esr->jer/dot_general | solution.py:41
  62.5 1.4 fusion.72
  63.9 1.1 pad_maximum_fusion
  65.0 1.5 copy.15
  66.5 20.9 %all_to_all.18 = bf16[512,8,128]{2,1,0:T(8,128)(2,1)S(1)} all-to-all(bf16[512,8,128]{2,1,0:T(8,128)(2,1)} %copy.15), channel_id=1, replica_groups=mesh['dp'=16,'tensor'=8] {'dp'}, dimensions={0} | all-to-all | bytes 2097152 | tf_op jit(solution)/shard_map/all_to_all | solution.py:45
  87.4 0.0 slice-start
  87.4 0.0 slice-start.1
  87.4 0.0 slice-start.2
  87.4 9.6 %fusion.27 = f32[128,8192]{1,0:T(8,128)} fusion(s32[1,32,128,1024]{3,2,1,0:T(8,128)} %param.13, bf16[32,16,8,128]{3,2,0,1:T(8,128)(2,1)S(1)} %bitcast.135), kind=kOutput, calls=%fused_computation.27 | convolution fusion | flops 1094713344 | bytes 18350080 | tf_op jit(solution)/shard_map/dot_general | solution.py:53
  97.0 0.0 slice-start.3
  97.0 10.2 %fusion.33 = f32[128,8192]{1,0:T(8,128)} fusion(f32[128,8192]{1,0:T(8,128)} %fusion.27, s32[1,32,128,1024]{3,2,1,0:T(8,128)} %param.13, bf16[32,16,8,128]{3,2,0,1:T(8,128)(2,1)S(1)} %bitcast.136), kind=kOutput, calls=%fused_computation.29 | convolution fusion | flops 1094713344 | bytes 18350080 | tf_op jit(solution)/shard_map/dot_general | solution.py:53
  107.2 0.0 slice-done
  107.2 0.0 slice-done.1
  107.2 0.0 slice-done.2
  107.2 0.0 slice-done.3
  107.2 4.3 %fusion.39 = f32[128,8192]{1,0:T(8,128)} fusion(f32[128,8192]{1,0:T(8,128)} %fusion.33, s32[1,32,128,1024]{3,2,1,0:T(8,128)S(1)} %bitcast.144, bf16[32,16,8,128]{3,2,0,1:T(8,128)(2,1)S(1)} %bitcast.137), kind=kOutput, calls=%fused_computation.31 | convolution fusion | flops 1094713344 | bytes 18350080 | tf_op jit(solution)/shard_map/dot_general | solution.py:53
  111.4 4.5 %fusion.45 = f32[128,8192]{1,0:T(8,128)} fusion(f32[128,8192]{1,0:T(8,128)} %fusion.39, s32[1,32,128,1024]{3,2,1,0:T(8,128)S(1)} %bitcast.144, bf16[32,16,8,128]{3,2,0,1:T(8,128)(2,1)S(1)} %bitcast.138), kind=kOutput, calls=%fused_computation.33 | convolution fusion | flops 1094713344 | bytes 18350080 | tf_op jit(solution)/shard_map/dot_general | solution.py:53
  115.9 4.2 %fusion.51 = f32[128,8192]{1,0:T(8,128)} fusion(f32[128,8192]{1,0:T(8,128)} %fusion.45, s32[1,32,128,1024]{3,2,1,0:T(8,128)S(1)} %bitcast.144, bf16[32,16,8,128]{3,2,0,1:T(8,128)(2,1)S(1)} %bitcast.139), kind=kOutput, calls=%fused_computation.35 | convolution fusion | flops 1094713344 | bytes 18350080 | tf_op jit(solution)/shard_map/dot_general | solution.py:53
  120.2 4.2 %fusion.57 = f32[128,8192]{1,0:T(8,128)} fusion(f32[128,8192]{1,0:T(8,128)} %fusion.51, s32[1,32,128,1024]{3,2,1,0:T(8,128)S(1)} %bitcast.144, bf16[32,16,8,128]{3,2,0,1:T(8,128)(2,1)S(1)} %bitcast.140), kind=kOutput, calls=%fused_computation.37 | convolution fusion | flops 1094713344 | bytes 18350080 | tf_op jit(solution)/shard_map/dot_general | solution.py:53
  124.4 4.2 %fusion.63 = f32[128,8192]{1,0:T(8,128)} fusion(f32[128,8192]{1,0:T(8,128)} %fusion.57, s32[1,32,128,1024]{3,2,1,0:T(8,128)S(1)} %bitcast.144, bf16[32,16,8,128]{3,2,0,1:T(8,128)(2,1)S(1)} %bitcast.141), kind=kOutput, calls=%fused_computation.39 | convolution fusion | flops 1094713344 | bytes 18350080 | tf_op jit(solution)/shard_map/dot_general | solution.py:53
  128.7 0.0 copy-start.2
  128.7 4.5 %fusion.69 = f32[128,8192]{1,0:T(8,128)} fusion(f32[128,8192]{1,0:T(8,128)} %fusion.63, s32[1,32,128,1024]{3,2,1,0:T(8,128)S(1)} %bitcast.144, bf16[32,16,8,128]{3,2,0,1:T(8,128)(2,1)S(1)} %bitcast.142), kind=kOutput, calls=%fused_computation.41 | convolution fusion | flops 1094713344 | bytes 18350080 | tf_op jit(solution)/shard_map/dot_general | solution.py:53
  133.2 0.0 all-reduce.4.cloned.1.call-update
  133.2 0.0 copy-done
  133.2 0.0 copy-done.2
  133.2 1.9 fusion.101
  135.1 147.0 %all-reduce.4.cloned.1.call-done = f32[128,8192]{1,0:T(8,128)} async-done(((f32[128,8192]{1,0:T(8,128)}), f32[128,8192]{1,0:T(8,128)}) %all-reduce.4.cloned.1.call-update) | async-done | bytes 4194320
  282.0 1.6 multiply_reduce_fusion
  284.3 1.0 dynamic-slice_multiply_fusion
  285.3 0.0 copy-start.1
  285.3 3.9 %fusion.75 = f32[1,64]{1,0:T(1,128)} fusion(f32[64,8192]{1,0:T(8,128)} %fusion.101, f32[1,8192]{1,0:T(1,128)S(1)} %dynamic-slice_multiply_fusion), kind=kOutput, calls=%fused_computation.47 | convolution fusion | flops 6291520 | bytes 2130176 | tf_op jit(solution)/shard_map/dot_general | solution.py:65
  289.2 0.0 copy-done.1
  (1 shorter events, 0.0 us)
Async XLA Ops:
  7.2 126.0 %copy-start = (bf16[128,8192]{1,0:T(8,128)(2,1)S(1)}, bf16[128,8192]{1,0:T(8,128)(2,1)}, u32[]{:S(2)}) copy-start(bf16[128,8192]{1,0:T(8,128)(2,1)} %param.14) | copy-start | bytes 6291460
  7.2 274.8 %all-reduce.4.cloned.1.call-start = ((), (), s32[]{:S(2)}) async-start(), calls=%async_computation.1 | async-start | bytes 8388608
  87.4 19.8 %slice-start = ((s8[16777216]{0:T(1024)(128)(4,1)}), s8[4194304]{0:T(1024)(128)(4,1)S(1)}, s32[]{:S(2)}) async-start(s8[16777216]{0:T(1024)(128)(4,1)} %bitcast.143), calls=%async_computation.2 | async-start | bytes 8388608
  87.4 19.8 %slice-start.1 = ((s8[16777216]{0:T(1024)(128)(4,1)}), s8[4194304]{0:T(1024)(128)(4,1)S(1)}, s32[]{:S(2)}) async-start(s8[16777216]{0:T(1024)(128)(4,1)} %bitcast.143), calls=%async_computation.3 | async-start | bytes 8388608
  87.4 19.8 %slice-start.2 = ((s8[16777216]{0:T(1024)(128)(4,1)}), s8[4194304]{0:T(1024)(128)(4,1)S(1)}, s32[]{:S(2)}) async-start(s8[16777216]{0:T(1024)(128)(4,1)} %bitcast.143), calls=%async_computation.4 | async-start | bytes 8388608
  97.0 10.2 %slice-start.3 = ((s8[16777216]{0:T(1024)(128)(4,1)}), s8[4194304]{0:T(1024)(128)(4,1)S(1)}, s32[]{:S(2)}) async-start(s8[16777216]{0:T(1024)(128)(4,1)} %bitcast.143), calls=%async_computation.5 | async-start | bytes 8388608
  128.7 4.5 %copy-start.2 = (s32[64]{0:T(128)S(1)}, s32[64]{0:T(128)}, u32[]{:S(2)}) copy-start(s32[64]{0:T(128)} %param.15) | copy-start | bytes 772
  285.3 3.9 %copy-start.1 = (f32[1,8192]{1,0:T(1,128)}, f32[1,8192]{1,0:T(1,128)S(1)}, u32[]{:S(2)}) copy-start(f32[1,8192]{1,0:T(1,128)S(1)} %dynamic-slice_multiply_fusion) | copy-start | bytes 98308
Sparse Core Ops, SparseCore 0:
  133.3 148.6 all-reduce.3
where the time goes:
time: 297 us; the launch traced here: 296 us
  waiting for transfers between devices  147 us (49%)
  blocking collectives  68.9 us (23%)
  matrix products  59.2 us (20%)
  between operations  14.8 us (5%)
  other arithmetic  4.61 us (2%)
    unnamed x2, waiting for transfers between devices  147 us
    psum x1, blocking collectives, per_device(): coupled_gradient = lax.psum(partial_u, 'tensor').astype(jnp.bfloat16)  48.1 us
    dot_general x8, matrix products, per_device(): lax.dot_general(moved, sign_block, (((0, 2), (0, 1)), ((), ())), preferre...  45.8 us
    all_to_all x1, blocking collectives, per_device(): lax.all_to_all(gradient, 'dp', split_axis=0, concat_axis=1, tiled=True)  20.9 us
  transfers between devices with their start and end apart: 1, of which 1 were waited for; matrix products, arithmetic and copies ran while one was open for 1% of the time, Pallas kernels for 0%

commit v1 on v0

v1 whole, which is shorter than its diff:
```python
import math

import jax
import jax.numpy as jnp
from jax import lax
from jax.experimental import pallas as pl
from jax.experimental.pallas import tpu as pltpu
from jax.sharding import PartitionSpec as P

BF16 = jnp.bfloat16
F32 = jnp.float32
MESH = pl.DeviceIdType.MESH

NDP = 16
NT = 8
EPD = 8
SEQ = 64
RANK = 64
WIDTH = 4096
SLICE = 512
ROWS = 32
WORDS = 1024
NS = 4
SW = WORDS // NS
HALFK = ROWS * RANK
AXES = ("x", "z", "x", "z")


def dot(a, b, dims=(((1,), (0,)), ((), ()))):
    return lax.dot_general(a, b, dims, preferred_element_type=F32)


def body(
    acts_hbm, og_hbm, down_hbm, up_hbm, counts, signs_hbm, bank_hbm, vrows_hbm,
    feat_out, score_out,
    acts, mg, down2, up, bank, vrows, words, nib,
    pu, pu_recv, cpl_recv, cpl4, hid4,
    sb, rb, trans, grad, acc, rowsum,
    part, s0, r0, s1, r1, k1, s2, r2, feat,
    in_sem, word_sem, own_sem, snd, rcv,
):
    d = lax.axis_index("dp")
    t = lax.axis_index("tensor")
    x = d // 4
    y_lo = (d // 2) % 2
    core = d % 2
    z = t // 2
    y_hi = t % 2

    def load(src, dst, n):
        c = pltpu.make_async_copy(src, dst, in_sem.at[n])
        c.start()
        return c

    c_og = load(og_hbm, mg, 0)
    c_up = load(up_hbm, up, 1)
    c_down = [load(down_hbm, down2.at[pl.ds(i * RANK, RANK)], 2 + i) for i in range(2)]
    c_acts = [
        load(acts_hbm.at[pl.ds(i * 128, 128)], acts.at[pl.ds(i * 128, 128)], 4 + i) for i in range(4)
    ]
    c_words = []
    for i in range(8):
        c = pltpu.make_async_copy(
            signs_hbm.at[pl.ds(i * 4, 4)], words.at[pl.ds(i * 4, 4)], word_sem.at[i]
        )
        c.start()
        c_words.append(c)
    c_bank = load(bank_hbm, bank, 8)
    c_vrows = load(vrows_hbm, vrows, 9)

    barrier = pltpu.get_barrier_semaphore()

    def greet(dd, tt):
        pl.semaphore_signal(
            barrier, inc=1, device_id={"dp": dd, "tensor": tt}, device_id_type=MESH
        )

    for k in range(1, NDP):
        greet((d + k) % NDP, t)
    for k in range(1, NT):
        greet(d, (t + k) % NT)
    d_flip = d + 2 - 4 * y_lo
    t_flip = t + 1 - 2 * y_hi
    for k in range(1, NT):
        greet(d_flip, (t + k) % NT)
    for k in range(1, 8):
        m = (x * 2 + y_lo + k) % 8
        greet(m * 2 + core, t_flip)

    lane = lax.broadcasted_iota(jnp.int32, (1, 128), 1)
    low = lane < 64

    def split4(v):
        zero = jnp.zeros_like(v)
        return jnp.concatenate([jnp.where(low, v, zero), jnp.where(low, zero, v)], axis=1)

    c_og.wait()
    token = lax.broadcasted_iota(jnp.int32, (SEQ, SLICE), 0)
    for e in range(EPD):
        rows = pl.ds(e * SEQ, SEQ)
        v = mg[rows, :].astype(F32)
        mg[rows, :] = jnp.where(token < counts[e], v, 0.0).astype(BF16)

    c_up.wait()
    eye2 = (
        lax.broadcasted_iota(jnp.int32, (RANK, 128), 1) % RANK
        == lax.broadcasted_iota(jnp.int32, (RANK, 128), 0)
    ).astype(F32).astype(BF16)
    up4 = split4(dot(up[...], eye2)).astype(BF16)
    pu[...] = (
        dot(mg[0:256, :], up4[:, 0:128]) + dot(mg[256:512, :], up4[:, 128:256])
    )

    pl.semaphore_wait(barrier, 36)

    def send_pu(k, _):
        tt = (t + k) % NT
        pltpu.make_async_remote_copy(
            src_ref=pu.at[pl.ds(pl.multiple_of(tt * 32, 32), 32)],
            dst_ref=pu_recv.at[k - 1],
            send_sem=snd.at[0],
            recv_sem=rcv.at[0],
            device_id={"dp": d, "tensor": tt},
            device_id_type=MESH,
        ).start()
        return 0

    lax.fori_loop(1, NT, send_pu, 0)

    for c in c_down:
        c.wait()
    for i in range(4):
        c_acts[i].wait()
        rows = pl.ds(i * 128, 128)
        h = dot(acts[rows, :], down2[...], (((1,), (1,)), ((), ())))
        hid4[rows, :] = split4(h).astype(BF16)

    def outer(lhs, rhs, half):
        def one(e, _):
            rows = pl.ds(pl.multiple_of(e * SEQ, SEQ), SEQ)
            o = dot(lhs(rows), rhs[rows, :], (((0,), (0,)), ((), ())))
            o = o.reshape(NDP, 2, 16, 256)
            g = o[:, 0, :, 0:128] + o[:, 1, :, 128:256]
            sb[half, :, e] = g.astype(BF16)
            return 0

        lax.fori_loop(0, EPD, one, 0)

    def send_grad(half):
        def one(k, _):
            dd = (d + k) % NDP
            pltpu.make_async_remote_copy(
                src_ref=sb.at[half, dd],
                dst_ref=rb.at[half, d],
                send_sem=snd.at[2 + half],
                recv_sem=rcv.at[2 + half],
                device_id={"dp": dd, "tensor": t},
                device_id_type=MESH,
            ).start()
            return 0

        lax.fori_loop(1, NDP, one, 0)
        own = pltpu.make_async_copy(sb.at[half, d], rb.at[half, d], own_sem.at[half])
        own.start()
        return own

    def wait_bytes(ref, sem):
        pltpu.make_async_copy(ref, ref, sem).wait()

    outer(lambda rows: mg[rows, :], hid4, 1)
    own_b = send_grad(1)

    wait_bytes(pu_recv, rcv.at[0])
    total = pu[pl.ds(pl.multiple_of(t * 32, 32), 32), :]
    for k in range(NT - 1):
        total = total + pu_recv[k]
    cpl_recv[t] = total.astype(BF16)

    def send_cpl(k, _):
        tt = (t + k) % NT
        pltpu.make_async_remote_copy(
            src_ref=cpl_recv.at[t],
            dst_ref=cpl_recv.at[t],
            send_sem=snd.at[1],
            recv_sem=rcv.at[1],
            device_id={"dp": d, "tensor": tt},
            device_id_type=MESH,
        ).start()
        return 0

    lax.fori_loop(1, NT, send_cpl, 0)

    def convert(half, hi):
        def one(jp, _):
            w = words[jp + 16 * hi, pl.ds(half * RANK, RANK), :]
            rows = pl.ds(hi * RANK, RANK)
            quarter = jnp.asarray(0.25, BF16)
            nib[0, half, jp, rows, :] = (w & 15).astype(F32).astype(BF16) + quarter
            nib[1, half, jp, rows, :] = (w >> 4).astype(F32).astype(BF16) + quarter
            return 0

        lax.fori_loop(0, 16, one, 0)

    for c in c_words:
        c.wait()
    convert(1, 0)

    wait_bytes(cpl_recv.at[pl.ds(0, NT - 1)], rcv.at[1])
    v = cpl_recv[...].reshape(256, 128).astype(F32)
    w = pltpu.roll(v, 64, 1)
    zero = jnp.zeros_like(v)
    cpl4[0:256, 0:128] = jnp.where(low, v, zero).astype(BF16)
    cpl4[0:256, 128:256] = jnp.where(low, zero, w).astype(BF16)
    cpl4[256:512, 0:128] = jnp.where(low, w, zero).astype(BF16)
    cpl4[256:512, 128:256] = jnp.where(low, zero, v).astype(BF16)
    offset = pl.multiple_of(t * SLICE, SLICE)
    outer(lambda rows: acts[rows, pl.ds(offset, SLICE)], cpl4, 0)
    own_a = send_grad(0)

    convert(1, 1)
    convert(0, 0)
    convert(0, 1)

    ones = jnp.ones((HALFK, 128), BF16)

    def gather(half, own):
        own.wait()
        wait_bytes(rb.at[half, pl.ds(0, NDP - 1)], rcv.at[2 + half])
        trans[...] = rb[half].reshape(2048, 128).astype(F32)
        for jp in range(16):
            grad[half, :, jp * 128:(jp + 1) * 128] = trans[
                pl.ds(jp, 128, stride=16), :
            ].astype(BF16)

    def planes(half, s):
        g = grad[half]
        cols = pl.ds(s * SW, SW) if isinstance(s, int) else pl.ds(pl.multiple_of(s * SW, SW), SW)
        out = []
        for q in range(2):
            n = nib[q, half, :, :, cols].reshape(HALFK, SW)
            res = [dot(g, n)]
            for k in (4, 3, 2):
                shift = jnp.asarray(2.0 ** (7 + k), BF16)
                res.append(dot(g, (n + shift) - shift))
            out.append(res)
        return out

    gather(1, own_b)
    rowsum[...] = dot(grad[1], ones)

    def first(s, _):
        got = planes(1, s)
        for q in range(2):
            for i in range(4):
                acc[s, q, i] = got[q][i]
        return 0

    lax.fori_loop(0, NS, first, 0)

    gather(0, own_a)
    rowsum[...] += dot(grad[0], ones)

    def compute(s):
        got = planes(0, s)
        r = rowsum[...]
        for h in range(SW // 128):
            cols = slice(h * 128, (h + 1) * 128)
            for q in range(2):
                d0, d4, d3, d2 = (got[q][i][:, cols] + acc[s, q, i, :, cols] for i in range(4))
                a4, a3 = d4 * 0.125, d3 * 0.25
                p3 = a4 - r
                p2 = a3 - a4 - r
                p1 = d2 * 0.5 - a3 - a4 - r
                p0 = 2.0 * d0 - d2 - 2.0 * a3 - 2.0 * a4 - 1.5 * r
                for i, p in enumerate((p0, p1, p2, p3)):
                    row = h * 8 + q * 4 + i
                    for dd in range(NDP):
                        v = p[dd * 8:(dd + 1) * 8, :]
                        if AXES[s] == "x":
                            base = (dd % 2) * 64 + (dd // 2) * 8
                            where = pl.ds(base * 16 + row, 8, stride=16)
                        else:
                            base = (dd % 2) * 64 + dd // 2
                            where = pl.ds(base * 16 + row, 8, stride=128)
                        part[s, where, :] = v
        theirs = pl.ds(pl.multiple_of((1 - core) * 1024, 1024), 1024)
        s0[s] = part[s, theirs, :].astype(BF16)
        pltpu.make_async_remote_copy(
            src_ref=s0.at[s],
            dst_ref=r0.at[s],
            send_sem=snd.at[4 + 3 * s],
            recv_sem=rcv.at[4 + 3 * s],
            device_id={"dp": d + 1 - 2 * core, "tensor": t},
            device_id_type=MESH,
        ).start()

    def along(s):
        wait_bytes(r0.at[s], rcv.at[4 + 3 * s])
        a = x if AXES[s] == "x" else z
        for k in (1, 2, 3, 0):
            g = (a + k) % 4
            mine = pl.ds(pl.multiple_of(core * 1024 + g * 256, 256), 256)
            v = part[s, mine, :] + r0[s, pl.ds(pl.multiple_of(g * 256, 256), 256), :].astype(F32)
            if k == 0:
                k1[s] = v
                continue
            s1[s, k - 1] = v.astype(BF16)
            if AXES[s] == "x":
                peer = {"dp": g * 4 + d % 4, "tensor": t}
            else:
                peer = {"dp": d, "tensor": g * 2 + y_hi}
            pltpu.make_async_remote_copy(
                src_ref=s1.at[s, k - 1],
                dst_ref=r1.at[s, k - 1],
                send_sem=snd.at[5 + 3 * s],
                recv_sem=rcv.at[5 + 3 * s],
                device_id=peer,
                device_id_type=MESH,
            ).start()

    def place(s):
        if AXES[s] == "x":
            return y_lo * 8 + t
        return y_hi * 8 + x * 2 + y_lo

    def across(s):
        wait_bytes(r1.at[s], rcv.at[5 + 3 * s])
        v = k1[s]
        for k in range(3):
            v = v + r1[s, k].astype(F32)
        s2[s] = v.reshape(16, 16, 128)
        m = place(s)

        def one(k, _):
            mm = (m + k) % 16
            if AXES[s] == "x":
                peer = {"dp": x * 4 + (mm // 8) * 2 + core, "tensor": mm % 8}
            else:
                peer = {"dp": (mm % 8) * 2 + core, "tensor": z * 2 + mm // 8}
            pltpu.make_async_remote_copy(
                src_ref=s2.at[s, mm],
                dst_ref=r2.at[s, k - 1],
                send_sem=snd.at[6 + 3 * s],
                recv_sem=rcv.at[6 + 3 * s],
                device_id=peer,
                device_id_type=MESH,
            ).start()
            return 0

        lax.fori_loop(1, 16, one, 0)

    def owned(s, score):
        wait_bytes(r2.at[s], rcv.at[6 + 3 * s])
        v = s2[s, place(s)]
        for k in range(15):
            v = v + r2[s, k]
        for h in range(2):
            feat[pl.ds(s * 2 + h, 8, stride=8), :] = v[h * 8:(h + 1) * 8, :]
            for b in range(8):
                cols = b * WORDS + s * SW + h * 128
                score = score + v[h * 8 + b:h * 8 + b + 1, :] * bank[:, cols:cols + 128].astype(F32)
        return score

    compute(0)
    compute(1)
    along(0)
    compute(2)
    along(1)
    compute(3)
    along(2)
    across(0)
    along(3)
    across(1)
    across(2)
    c_bank.wait()
    c_vrows.wait()
    score = jnp.zeros((128, 128), F32)
    score = owned(0, score)
    score = owned(1, score)
    across(3)
    score = owned(2, score)
    score = owned(3, score)

    f = feat[...]
    mean = jnp.sum(f * f, keepdims=True) * (1.0 / (8 * WORDS))
    inv = lax.rsqrt(mean + 1e-06)
    feat_out[...] = f * inv
    by_row = jnp.sum(score, axis=1, keepdims=True)
    pick = lax.broadcasted_iota(jnp.int32, (128, 64), 0) == vrows[...]
    chosen = jnp.sum(jnp.where(pick, by_row, 0.0), axis=0, keepdims=True)
    score_out[...] = chosen * inv * (1.0 / math.sqrt(8 * WORDS))

    wait_bytes(pu_recv, snd.at[0])
    wait_bytes(cpl_recv.at[pl.ds(0, NT - 1)], snd.at[1])
    for half in range(2):
        wait_bytes(sb.at[half, pl.ds(0, NDP - 1)], snd.at[2 + half])
    for s in range(NS):
        wait_bytes(s0.at[s], snd.at[4 + 3 * s])
        wait_bytes(s1.at[s], snd.at[5 + 3 * s])
        wait_bytes(s2.at[s, pl.ds(0, 15)], snd.at[6 + 3 * s])


def per_device(acts, og, down, up, counts, signs, bank, vrows):
    anywhere = pl.BlockSpec(memory_space=pl.ANY)
    vmem = pltpu.VMEM
    feat, score = pl.pallas_call(
        body,
        out_shape=(
            jax.ShapeDtypeStruct((64, 128), F32),
            jax.ShapeDtypeStruct((1, 64), F32),
        ),
        in_specs=[
            anywhere, anywhere, anywhere, anywhere,
            pl.BlockSpec(memory_space=pltpu.SMEM),
            anywhere, anywhere, anywhere,
        ],
        out_specs=(pl.BlockSpec(memory_space=pltpu.VMEM),) * 2,
        scratch_shapes=[
            vmem((EPD * SEQ, WIDTH), BF16),
            vmem((EPD * SEQ, SLICE), BF16),
            vmem((2 * RANK, WIDTH), BF16),
            vmem((SLICE, RANK), BF16),
            vmem((128, 8 * WORDS), BF16),
            vmem((1, 64), jnp.int32),
            vmem((ROWS, 128, WORDS), jnp.int32),
            vmem((2, 2, 16, 128, WORDS), BF16),
            vmem((256, 128), F32),
            vmem((NT - 1, 32, 128), F32),
            vmem((NT, 32, 128), BF16),
            vmem((EPD * SEQ, 256), BF16),
            vmem((EPD * SEQ, 256), BF16),
            vmem((2, NDP, EPD, 16, 128), BF16),
            vmem((2, NDP, EPD, 16, 128), BF16),
            vmem((2048, 128), F32),
            vmem((2, 128, HALFK), BF16),
            vmem((NS, 2, 4, 128, SW), F32),
            vmem((128, 128), F32),
            vmem((NS, 2048, 128), F32),
            vmem((NS, 1024, 128), BF16),
            vmem((NS, 1024, 128), BF16),
            vmem((NS, 3, 256, 128), BF16),
            vmem((NS, 3, 256, 128), BF16),
            vmem((NS, 256, 128), F32),
            vmem((NS, 16, 16, 128), F32),
            vmem((NS, 15, 16, 128), F32),
            vmem((64, 128), F32),
            pltpu.SemaphoreType.DMA((10,)),
            pltpu.SemaphoreType.DMA((8,)),
            pltpu.SemaphoreType.DMA((2,)),
            pltpu.SemaphoreType.DMA((4 + 3 * NS,)),
            pltpu.SemaphoreType.DMA((4 + 3 * NS,)),
        ],
        compiler_params=pltpu.CompilerParams(
            collective_id=0, has_side_effects=True, vmem_limit_bytes=63 << 20
        ),
    )(
        acts.reshape(EPD * SEQ, WIDTH),
        og.reshape(EPD * SEQ, SLICE),
        down,
        up,
        counts,
        signs.reshape(ROWS, 128, WORDS),
        bank,
        vrows.reshape(1, 64),
    )
    return feat.reshape(1, 8 * WORDS), score


def solution(mesh):
    in_specs = (
        P("dp", None, None),
        P("dp", None, "tensor"),
        P(),
        P("tensor", None),
        P("dp"),
        P("tensor", "dp", None, None),
        P(),
        P(),
    )
    out_specs = (P(("dp", "tensor"), None), P(("dp", "tensor"), None))
    return jax.shard_map(
        per_device, mesh=mesh, in_specs=in_specs, out_specs=out_specs, check_vma=False
    )
```

time: 297 us -> 63 us (0.21)
  waiting for transfers between devices: 147 us -> 0 us
  blocking collectives: 68.9 us -> 0 us
  matrix products: 59.2 us -> 0 us
  Pallas kernels: 0 us -> 58.1 us
  between operations: 14.8 us -> 0.64 us
  other arithmetic: 4.61 us -> 0 us
    unnamed x2 -> x0, waiting for transfers between devices: 147 us -> none
    dot_general x13 -> x0, matrix products: 59.2 us -> none  [the longest x8 45.8 us: per_device(): lax.dot_general(moved, sign_block, (((0, 2), (0, 1)), ((), ())), preferre...]
    pallas_call x0 -> x1, Pallas kernels: none -> 58.1 us  [per_device(): pl.pallas_call(body, out_shape=(jax.ShapeDtypeStruct((64, 128), F32), jax...]
    psum x1 -> x0, blocking collectives: 48.1 us -> none  [per_device(): coupled_gradient = lax.psum(partial_u, 'tensor').astype(jnp.bfloat16)]
    all_to_all x1 -> x0, blocking collectives: 20.9 us -> none  [per_device(): lax.all_to_all(gradient, 'dp', split_axis=0, concat_axis=1, tiled=True)]
    unnamed x14 -> x3, local copies, waits for them, and re-layouts: 0.03 us -> 4.1 us
  transfers between devices with their start and end apart: 1 -> 0, of which waited for: 1 -> 0; matrix products, arithmetic and copies ran while one was open for 1% -> 0% of each run, Pallas kernels for 0% -> 0%
where the time goes in v1:
time: 63 us; the launch traced here: 62.8 us
  Pallas kernels  58.1 us (92%)
  local copies, waits for them, and re-layouts  4.1 us (7%)
  between operations  0.64 us (1%)
    pallas_call x1, Pallas kernels, per_device(): pl.pallas_call(body, out_shape=(jax.ShapeDtypeStruct((64, 128), F32), jax...  58.1 us
    unnamed x3, local copies, waits for them, and re-layouts  4.1 us

profile of v1, /device:TPU:0, one launch (start us, length us, event | category | flops | bytes accessed | tf_op | source)
XLA Modules:
  0.0 62.8 jit_solution(14966764133675966533)
XLA Ops:
  0.6 1.6 %copy.10.up_hbm = bf16[512,64]{1,0:T(8,128)(2,1)} copy(bf16[512,64]{0,1:T(8,128)(2,1)} %param.11) | data formatting | bytes 131072 | tf_op args[3]
  2.2 58.1 %shard_map.95 = (f32[64,128]{1,0:T(8,128)}, f32[1,64]{1,0:T(1,128)}) custom-call(bf16[512,4096]{1,0:T(8,128)(2,1)} %bitcast.6, bf16[512,512]{1,0:T(8,128)(2,1)} %bitcast.7, bf16[64,4096]{1,0:T(8,128)(2,1)} %down_hbm.1, bf16[512,64]{1,0:T(8,128)(2,1)} %copy.10.up_hbm, s32[8]{0:T(128)} %counts.1, s32[32,128,1024]{2,1,0:T(8,128)} %bitcast.5, ...), custom_call_target="tpu_custom_call" | custom-call | tf_op jit(solution)/shard_map/pallas_call | solution.py:406
  60.3 1.4 %copy.13 = f32[1,8192]{1,0:T(1,128)} copy(f32[1,8192]{1,0:T(1,128)} %bitcast.8) | data formatting | bytes 65536
  61.7 1.1 %copy.14 = f32[1,64]{1,0:T(1,128)} copy(f32[1,64]{1,0:T(1,128)} %get-tuple-element.9) | data formatting | bytes 512

commit v2 on v1

v2 whole, which is shorter than its diff:
```python
import math

import jax
import jax.numpy as jnp
from jax import lax
from jax.experimental import pallas as pl
from jax.experimental.pallas import tpu as pltpu
from jax.sharding import PartitionSpec as P

BF16 = jnp.bfloat16
F32 = jnp.float32
MESH = pl.DeviceIdType.MESH

NDP = 16
NT = 8
EPD = 8
SEQ = 64
RANK = 64
WIDTH = 4096
SLICE = 512
ROWS = 32
WORDS = 1024
CHUNK = 1024
PARTS = ((1, 0), (1, 1), (0, 0), (0, 1))
AXES = ("x", "z", "y", "x", "z")
WIDTHS = (256, 256, 256, 128, 128)
NS = len(AXES)
STARTS = tuple(sum(WIDTHS[:s]) for s in range(NS))
PER = tuple(w // 16 for w in WIDTHS)
BEFORE = tuple(w // 16 for w in STARTS)


def dot(a, b, dims=(((1,), (0,)), ((), ()))):
    return lax.dot_general(a, b, dims, preferred_element_type=F32)


def body(
    acts_hbm, og_hbm, down_hbm, up_hbm, counts, signs_hbm, bank_hbm, vrows_hbm,
    out,
    acts, mg, down2, up2, bank, vrows, words, nib,
    pu, pu_recv, cpl_recv, cpl4, hid4,
    sb, rb, trans, grad, acc, rowsum,
    part, s0, r0, s1, r1, k1, s2b, r2b, s2f, r2f, feat,
    in_sem, word_sem, own_sem, snd, rcv,
):
    d = lax.axis_index("dp")
    t = lax.axis_index("tensor")
    x = d // 4
    y_lo = (d // 2) % 2
    core = d % 2
    z = t // 2
    y_hi = t % 2

    def load(src, dst, n):
        c = pltpu.make_async_copy(src, dst, in_sem.at[n])
        c.start()
        return c

    c_og = load(og_hbm, mg, 0)
    c_up = [load(up_hbm, up2.at[pl.ds(i * RANK, RANK)], 10 + i) for i in range(2)]
    c_down = [load(down_hbm, down2.at[pl.ds(i * RANK, RANK)], 2 + i) for i in range(2)]
    for i in range(4):
        load(acts_hbm.at[pl.ds(i * 128, 128)], acts.at[pl.ds(i * 128, 128)], 4 + i)

    barrier = pltpu.get_barrier_semaphore()

    def greet(dd, tt):
        pl.semaphore_signal(
            barrier, inc=1, device_id={"dp": dd, "tensor": tt}, device_id_type=MESH
        )

    for k in range(1, NDP):
        greet((d + k) % NDP, t)
    for k in range(1, NT):
        greet(d, (t + k) % NT)
    d_flip = d + 2 - 4 * y_lo
    t_flip = t + 1 - 2 * y_hi
    for k in range(1, NT):
        greet(d_flip, (t + k) % NT)
    for k in range(1, 8):
        m = (x * 2 + y_lo + k) % 8
        greet(m * 2 + core, t_flip)
    for k in range(1, 4):
        for i in range(1, 4):
            greet((d + 4 * k) % NDP, (t + 2 * i) % NT)

    lane = lax.broadcasted_iota(jnp.int32, (1, 128), 1)
    low = lane < 64

    def split4(v):
        zero = jnp.zeros_like(v)
        return jnp.concatenate([jnp.where(low, v, zero), jnp.where(low, zero, v)], axis=1)

    c_og.wait()
    token = lax.broadcasted_iota(jnp.int32, (SEQ, SLICE), 0)
    for e in range(EPD):
        rows = pl.ds(e * SEQ, SEQ)
        v = mg[rows, :].astype(F32)
        mg[rows, :] = jnp.where(token < counts[e], v, 0.0).astype(BF16)

    for c in c_up:
        c.wait()
    u = dot(mg[...], up2[...], (((1,), (1,)), ((), ())))
    pu[...] = jnp.where(low, u[0:256, :], u[256:512, :])

    pl.semaphore_wait(barrier, 45)

    def send_pu(k, _):
        tt = (t + k) % NT
        pltpu.make_async_remote_copy(
            src_ref=pu.at[pl.ds(pl.multiple_of(tt * 32, 32), 32)],
            dst_ref=pu_recv.at[k - 1],
            send_sem=snd.at[0],
            recv_sem=rcv.at[0],
            device_id={"dp": d, "tensor": tt},
            device_id_type=MESH,
        ).start()
        return 0

    lax.fori_loop(1, NT, send_pu, 0)

    for c in c_down:
        c.wait()
    def hidden(i, _):
        rows = pl.ds(pl.multiple_of(i * 128, 128), 128)
        pltpu.make_async_copy(acts_hbm.at[rows], acts.at[rows], in_sem.at[4 + i]).wait()
        h = dot(acts[rows, :], down2[...], (((1,), (1,)), ((), ())))
        hid4[rows, :] = split4(h).astype(BF16)
        return 0

    lax.fori_loop(0, 2, hidden, 0)
    c_words = []
    for n, (half, c) in enumerate(PARTS):
        for hi in range(2):
            at = pl.ds(16 * hi + 8 * c, 8), pl.ds(half * RANK, RANK)
            copy = pltpu.make_async_copy(signs_hbm.at[at], words.at[at], word_sem.at[2 * n + hi])
            copy.start()
            c_words.append(copy)
    c_bank = load(bank_hbm, bank, 8)
    c_vrows = load(vrows_hbm, vrows, 9)
    acc[...] = jnp.zeros_like(acc)
    rowsum[...] = jnp.zeros_like(rowsum)
    lax.fori_loop(2, 4, hidden, 0)

    def outer(lhs, rhs, half):
        def product(e):
            rows = pl.ds(pl.multiple_of(e * SEQ, SEQ), SEQ)
            o = dot(lhs(rows), rhs[rows, :], (((0,), (0,)), ((), ())))
            o = o.reshape(NDP, 2, 16, 256)
            return o[:, 0, :, 0:128] + o[:, 1, :, 128:256]

        def one(p, _):
            g0, g1 = product(2 * p), product(2 * p + 1)
            for c in range(2):
                g = jnp.concatenate([g0[:, c * 8:c * 8 + 8], g1[:, c * 8:c * 8 + 8]], axis=1)
                sb[2 * (1 - half) + c, :, pl.ds(pl.multiple_of(p * 16, 16), 16), :] = g.astype(BF16)
            return 0

        lax.fori_loop(0, EPD // 2, one, 0, unroll=True)

    def send_grad(n):
        def one(k, _):
            dd = (d + k) % NDP
            pltpu.make_async_remote_copy(
                src_ref=sb.at[n, dd],
                dst_ref=rb.at[n, d],
                send_sem=snd.at[2 + n],
                recv_sem=rcv.at[2 + n],
                device_id={"dp": dd, "tensor": t},
                device_id_type=MESH,
            ).start()
            return 0

        lax.fori_loop(1, NDP, one, 0)
        pltpu.make_async_copy(sb.at[n, d], rb.at[n, d], own_sem.at[n]).start()

    def wait_bytes(ref, sem):
        pltpu.make_async_copy(ref, ref, sem).wait()

    outer(lambda rows: mg[rows, :], hid4, 1)

    wait_bytes(pu_recv, rcv.at[0])
    total = pu[pl.ds(pl.multiple_of(t * 32, 32), 32), :]
    for k in range(NT - 1):
        total = total + pu_recv[k]
    cpl_recv[t] = total.astype(BF16)

    def send_cpl(k, _):
        tt = (t + k) % NT
        pltpu.make_async_remote_copy(
            src_ref=cpl_recv.at[t],
            dst_ref=cpl_recv.at[t],
            send_sem=snd.at[1],
            recv_sem=rcv.at[1],
            device_id={"dp": d, "tensor": tt},
            device_id_type=MESH,
        ).start()
        return 0

    lax.fori_loop(1, NT, send_cpl, 0)
    send_grad(0)
    send_grad(1)

    def convert(n):
        half, c = PARTS[n]
        quarter = jnp.asarray(0.25, BF16)
        for hi in range(2):
            c_words[2 * n + hi].wait()

            def one(k, _):
                w = words[8 * c + k + 16 * hi, pl.ds(half * RANK, RANK), :]
                rows = pl.ds(hi * RANK, RANK)
                nib[n, 0, k, rows, :] = (w & 15).astype(F32).astype(BF16) + quarter
                nib[n, 1, k, rows, :] = (w >> 4).astype(F32).astype(BF16) + quarter
                return 0

            lax.fori_loop(0, 8, one, 0)

    convert(0)
    convert(1)

    wait_bytes(cpl_recv.at[pl.ds(0, NT - 1)], rcv.at[1])
    v = cpl_recv[...].reshape(256, 128).astype(F32)
    w = pltpu.roll(v, 64, 1)
    zero = jnp.zeros_like(v)
    cpl4[0:256, 0:128] = jnp.where(low, v, zero).astype(BF16)
    cpl4[0:256, 128:256] = jnp.where(low, zero, w).astype(BF16)
    cpl4[256:512, 0:128] = jnp.where(low, w, zero).astype(BF16)
    cpl4[256:512, 128:256] = jnp.where(low, zero, v).astype(BF16)
    offset = pl.multiple_of(t * SLICE, SLICE)
    outer(lambda rows: acts[rows, pl.ds(offset, SLICE)], cpl4, 0)
    send_grad(2)
    send_grad(3)

    ones = jnp.ones((CHUNK, 128), BF16)

    def gather(n):
        pltpu.make_async_copy(sb.at[n, d], rb.at[n, d], own_sem.at[n]).wait()
        wait_bytes(rb.at[n, pl.ds(0, NDP - 1)], rcv.at[2 + n])
        trans[...] = rb[n].reshape(1024, 128).astype(F32)
        for jp in range(8):
            grad[:, jp * 128:(jp + 1) * 128] = trans[pl.ds(jp, 128, stride=8), :].astype(BF16)
        rowsum[...] += dot(grad[...], ones)

    def planes(n, cols, width):
        g = grad[...]
        for q in range(2):
            v = nib[n, q, :, :, cols].reshape(CHUNK, width)
            yield q, 0, dot(g, v)
            for i, k in enumerate((4, 3, 2)):
                shift = jnp.asarray(2.0 ** (7 + k), BF16)
                yield q, i + 1, dot(g, (v + shift) - shift)

    def accumulate(n, _):
        gather(n)
        for q, i, v in planes(n, pl.ds(0, WORDS), WORDS):
            acc[q, i] += v
        return 0

    accumulate(0, 0)
    convert(2)
    accumulate(1, 0)
    convert(3)
    accumulate(2, 0)
    gather(3)

    def compute(s):
        per, base = PER[s], BEFORE[s]
        got = {}
        for q, i, v in planes(3, pl.ds(STARTS[s], WIDTHS[s]), WIDTHS[s]):
            got[q, i] = v
        r = rowsum[...]
        for h in range(per // 8):
            at = slice(STARTS[s] + h * 128, STARTS[s] + (h + 1) * 128)
            for q in range(2):
                d0, d4, d3, d2 = (
                    got[q, i][:, h * 128:(h + 1) * 128] + acc[q, i, :, at] for i in range(4)
                )
                a4, a3 = d4 * 0.125, d3 * 0.25
                p3 = a4 - r
                p2 = a3 - a4 - r
                p1 = d2 * 0.5 - a3 - a4 - r
                p0 = 2.0 * d0 - d2 - 2.0 * a3 - 2.0 * a4 - 1.5 * r
                for i, p in enumerate((p0, p1, p2, p3)):
                    row = base * 128 + h * 8 + q * 4 + i
                    for dd in range(NDP):
                        if AXES[s] == "x":
                            e, step = dd // 2 * 8, 1
                        elif AXES[s] == "z":
                            e, step = dd // 2, 8
                        else:
                            e, step = dd // 2 % 2 * 32 + dd // 4, 4
                        e = e + dd % 2 * 64
                        part[pl.ds(e * per + row, 8, stride=step * per), :] = p[dd * 8:(dd + 1) * 8, :]
        half = 64 * per
        theirs = pl.ds(pl.multiple_of(base * 128 + (1 - core) * half, half), half)
        sent = pl.ds(base * 64, half)
        s0[sent, :] = part[theirs, :].astype(BF16)
        pltpu.make_async_remote_copy(
            src_ref=s0.at[sent],
            dst_ref=r0.at[sent],
            send_sem=snd.at[6 + 3 * s],
            recv_sem=rcv.at[6 + 3 * s],
            device_id={"dp": d + 1 - 2 * core, "tensor": t},
            device_id_type=MESH,
        ).start()

    def along(s):
        per, base = PER[s], BEFORE[s]
        group = 16 * per
        wait_bytes(r0.at[pl.ds(base * 64, 4 * group)], rcv.at[6 + 3 * s])
        a = {"x": x, "y": y_hi * 2 + y_lo, "z": z}[AXES[s]]
        for k in (1, 2, 3, 0):
            g = (a + k) % 4
            if AXES[s] == "y":
                pieces = [
                    (pl.multiple_of(((g % 2) * 4 + i) * 8 * per + (g // 2) * 4 * per, 4 * per), 4 * per)
                    for i in range(4)
                ]
            else:
                pieces = [(pl.multiple_of(g * group, group), group)]
            v = [
                part[pl.ds(pl.multiple_of(base * 128 + core * 4 * group + o, n), n), :]
                + r0[pl.ds(pl.multiple_of(base * 64 + o, n), n), :].astype(F32)
                for o, n in pieces
            ]
            v = v[0] if len(v) == 1 else jnp.concatenate(v, axis=0)
            if k == 0:
                k1[pl.ds(base * 16, group), :] = v
                continue
            sent = pl.ds(base * 48 + (k - 1) * group, group)
            s1[sent, :] = v.astype(BF16)
            if AXES[s] == "x":
                peer = {"dp": g * 4 + d % 4, "tensor": t}
            elif AXES[s] == "z":
                peer = {"dp": d, "tensor": g * 2 + y_hi}
            else:
                peer = {"dp": x * 4 + (g % 2) * 2 + core, "tensor": z * 2 + g // 2}
            pltpu.make_async_remote_copy(
                src_ref=s1.at[sent],
                dst_ref=r1.at[sent],
                send_sem=snd.at[7 + 3 * s],
                recv_sem=rcv.at[7 + 3 * s],
                device_id=peer,
                device_id_type=MESH,
            ).start()

    place = {"x": y_lo * 8 + t, "z": y_hi * 8 + x * 2 + y_lo, "y": z * 4 + x}

    def last_stage(s):
        if PER[s] == 16:
            return s2b, r2b, [i for i in range(NS) if PER[i] == 16].index(s)
        return s2f, r2f, [i for i in range(NS) if PER[i] == 8].index(s)

    def across(s):
        per, base = PER[s], BEFORE[s]
        group = 16 * per
        wait_bytes(r1.at[pl.ds(base * 48, 3 * group)], rcv.at[7 + 3 * s])
        v = k1[pl.ds(base * 16, group), :]
        for k in range(3):
            v = v + r1[pl.ds(base * 48 + k * group, group), :].astype(F32)
        k1[pl.ds(base * 16, group), :] = v
        have, into, n = last_stage(s)
        have[n] = v.reshape(16, per, 128).astype(have.dtype)
        m = place[AXES[s]]

        def one(k, _):
            mm = (m + k) % 16
            if AXES[s] == "x":
                peer = {"dp": x * 4 + (mm // 8) * 2 + core, "tensor": mm % 8}
            elif AXES[s] == "z":
                peer = {"dp": (mm % 8) * 2 + core, "tensor": z * 2 + mm // 8}
            else:
                peer = {"dp": (mm % 4) * 4 + d % 4, "tensor": (mm // 4) * 2 + y_hi}
            pltpu.make_async_remote_copy(
                src_ref=have.at[n, mm],
                dst_ref=into.at[n, k - 1],
                send_sem=snd.at[8 + 3 * s],
                recv_sem=rcv.at[8 + 3 * s],
                device_id=peer,
                device_id_type=MESH,
            ).start()
            return 0

        lax.fori_loop(1, 16, one, 0)

    def owned(s, score):
        per, base = PER[s], BEFORE[s]
        _, into, n = last_stage(s)
        wait_bytes(into.at[n], rcv.at[8 + 3 * s])
        v = k1[pl.ds(pl.multiple_of(base * 16 + place[AXES[s]] * per, per), per), :]
        for k in range(15):
            v = v + into[n, k].astype(F32)
        for h in range(per // 8):
            feat[pl.ds(STARTS[s] // 128 + h, 8, stride=8), :] = v[h * 8:(h + 1) * 8, :]

        def one(b, total):
            for h in range(per // 8):
                row = b * 8 + STARTS[s] // 128 + h
                cols = pl.ds(pl.multiple_of(row * 128, 128), 128)
                total = total + feat[pl.ds(row, 1), :] * bank[:, cols].astype(F32)
            return total

        score = lax.fori_loop(0, 8, one, score)
        return score

    compute(0)
    compute(1)
    compute(2)
    along(0)
    compute(3)
    along(1)
    compute(4)
    along(2)
    along(3)
    along(4)
    c_bank.wait()
    c_vrows.wait()
    for s in range(NS):
        across(s)
    score = jnp.zeros((128, 128), F32)
    for s in range(NS):
        score = owned(s, score)

    f = feat[...]
    mean = jnp.sum(f * f, keepdims=True) * (1.0 / (8 * WORDS))
    inv = lax.rsqrt(mean + 1e-06)
    out[0:64, :] = f * inv
    by_row = jnp.sum(score, axis=1, keepdims=True)
    pick = lax.broadcasted_iota(jnp.int32, (128, 64), 0) == vrows[...]
    chosen = jnp.sum(jnp.where(pick, by_row, 0.0), axis=0, keepdims=True)
    out[64:65, 0:64] = chosen * inv * (1.0 / math.sqrt(8 * WORDS))

    wait_bytes(pu_recv, snd.at[0])
    wait_bytes(cpl_recv.at[pl.ds(0, NT - 1)], snd.at[1])
    for n in range(4):
        wait_bytes(sb.at[n, pl.ds(0, NDP - 1)], snd.at[2 + n])
    for s in range(NS):
        group = 16 * PER[s]
        wait_bytes(s0.at[pl.ds(BEFORE[s] * 64, 4 * group)], snd.at[6 + 3 * s])
        wait_bytes(s1.at[pl.ds(BEFORE[s] * 48, 3 * group)], snd.at[7 + 3 * s])
        have, _, n = last_stage(s)
        wait_bytes(have.at[n, pl.ds(0, 15)], snd.at[8 + 3 * s])


def split(both, feat, score):
    feat[...] = both[0:64, :]
    score[...] = both[64:65, 0:64]


def per_device(acts, og, down, up, counts, signs, bank, vrows):
    anywhere = pl.BlockSpec(memory_space=pl.ANY)
    vmem = pltpu.VMEM
    both = pl.pallas_call(
        body,
        out_shape=jax.ShapeDtypeStruct((72, 128), F32),
        in_specs=[
            anywhere, anywhere, anywhere, anywhere,
            pl.BlockSpec(memory_space=pltpu.SMEM),
            anywhere, anywhere, anywhere,
        ],
        out_specs=pl.BlockSpec(memory_space=pltpu.VMEM),
        scratch_shapes=[
            vmem((EPD * SEQ, WIDTH), BF16),
            vmem((EPD * SEQ, SLICE), BF16),
            vmem((2 * RANK, WIDTH), BF16),
            vmem((2 * RANK, SLICE), BF16),
            vmem((128, 8 * WORDS), BF16),
            vmem((1, 64), jnp.int32),
            vmem((ROWS, 128, WORDS), jnp.int32),
            vmem((4, 2, 8, 128, WORDS), BF16),
            vmem((256, 128), F32),
            vmem((NT - 1, 32, 128), F32),
            vmem((NT, 32, 128), BF16),
            vmem((EPD * SEQ, 256), BF16),
            vmem((EPD * SEQ, 256), BF16),
            vmem((4, NDP, 64, 128), BF16),
            vmem((4, NDP, 64, 128), BF16),
            vmem((1024, 128), F32),
            vmem((128, CHUNK), BF16),
            vmem((2, 4, 128, WORDS), F32),
            vmem((128, 128), F32),
            vmem((128 * 64, 128), F32),
            vmem((64 * 64, 128), BF16),
            vmem((64 * 64, 128), BF16),
            vmem((48 * 64, 128), BF16),
            vmem((48 * 64, 128), BF16),
            vmem((16 * 64, 128), F32),
            vmem((3, 16, 16, 128), BF16),
            vmem((3, 15, 16, 128), BF16),
            vmem((2, 16, 8, 128), F32),
            vmem((2, 15, 8, 128), F32),
            vmem((64, 128), F32),
            pltpu.SemaphoreType.DMA((12,)),
            pltpu.SemaphoreType.DMA((8,)),
            pltpu.SemaphoreType.DMA((4,)),
            pltpu.SemaphoreType.DMA((6 + 3 * NS,)),
            pltpu.SemaphoreType.DMA((6 + 3 * NS,)),
        ],
        compiler_params=pltpu.CompilerParams(
            collective_id=0, has_side_effects=True, vmem_limit_bytes=63 << 20
        ),
    )(
        acts.reshape(EPD * SEQ, WIDTH),
        og.reshape(EPD * SEQ, SLICE),
        down,
        up.T,
        counts,
        signs.reshape(ROWS, 128, WORDS),
        bank,
        vrows.reshape(1, 64),
    )
    feat, score = pl.pallas_call(
        split,
        out_shape=(
            jax.ShapeDtypeStruct((64, 128), F32),
            jax.ShapeDtypeStruct((1, 64), F32),
        ),
    )(both)
    return feat.reshape(1, 8 * WORDS), score


def solution(mesh):
    in_specs = (
        P("dp", None, None),
        P("dp", None, "tensor"),
        P(),
        P("tensor", None),
        P("dp"),
        P("tensor", "dp", None, None),
        P(),
        P(),
    )
    out_specs = (P(("dp", "tensor"), None), P(("dp", "tensor"), None))
    return jax.shard_map(
        per_device, mesh=mesh, in_specs=in_specs, out_specs=out_specs, check_vma=False
    )
```

time: 63 us -> 52.7 us (0.84)
  Pallas kernels: 58.1 us -> 51.8 us
  local copies, waits for them, and re-layouts: 4.1 us -> 0 us
    pallas_call x1 -> x2, Pallas kernels: 58.1 us -> 51.8 us  [the longest x1 50.4 us: per_device(): pl.pallas_call(body, out_shape=jax.ShapeDtypeStruct((72, 128), F32), in_s...]
    unnamed x3 -> x0, local copies, waits for them, and re-layouts: 4.1 us -> none
where the time goes in v2:
time: 52.7 us; the launch traced here: 52.5 us
  Pallas kernels  51.8 us (98%)
  between operations  0.64 us (1%)
    pallas_call x1, Pallas kernels, per_device(): pl.pallas_call(body, out_shape=jax.ShapeDtypeStruct((72, 128), F32), in_s...  50.4 us
    pallas_call x1, Pallas kernels, per_device(): pl.pallas_call(split, out_shape=(jax.ShapeDtypeStruct((64, 128), F32), ja...  1.39 us

profile of v2, /device:TPU:0, one launch (start us, length us, event | category | flops | bytes accessed | tf_op | source)
XLA Modules:
  0.0 52.5 jit_solution(17521909237807383479)
XLA Ops:
  0.6 50.4 %shard_map.95.both = f32[72,128]{1,0:T(8,128)} custom-call(bf16[512,4096]{1,0:T(8,128)(2,1)} %bitcast.7, bf16[512,512]{1,0:T(8,128)(2,1)} %bitcast.8, bf16[64,4096]{1,0:T(8,128)(2,1)} %down_hbm.1, bf16[64,512]{1,0:T(8,128)(2,1)} %bitcast.9, s32[8]{0:T(128)} %counts.1, s32[32,128,1024]{2,1,0:T(8,128)} %bitcast.6, bf16[128,8192]{1,0:T(8,128)(2,1)} %bank_hbm.1, ...), custom_call_target="tpu_custom_call" | custom-call | tf_op jit(solution)/shard_map/pallas_call | solution.py:454
  51.1 1.4 %shard_map.96 = (f32[64,128]{1,0:T(8,128)}, f32[1,64]{1,0:T(1,128)}) custom-call(f32[72,128]{1,0:T(8,128)} %shard_map.95.both), custom_call_target="tpu_custom_call" | custom-call | tf_op jit(solution)/shard_map/pallas_call | solution.py:513

commit v3 on v2

--- a/solution.py
+++ b/solution.py
@@ -22,6 +22,7 @@
 WORDS = 1024
 CHUNK = 1024
 PARTS = ((1, 0), (1, 1), (0, 0), (0, 1))
+HOPS = (4, 12, 8, 2, 5, 13, 9, 3, 6, 14, 10, 1, 7, 15, 11)
 AXES = ("x", "z", "y", "x", "z")
 WIDTHS = (256, 256, 256, 128, 128)
 NS = len(AXES)
@@ -159,7 +160,7 @@
         lax.fori_loop(0, EPD // 2, one, 0, unroll=True)
 
     def send_grad(n):
-        def one(k, _):
+        for k in HOPS:
             dd = (d + k) % NDP
             pltpu.make_async_remote_copy(
                 src_ref=sb.at[n, dd],
@@ -169,9 +170,6 @@
                 device_id={"dp": dd, "tensor": t},
                 device_id_type=MESH,
             ).start()
-            return 0
-
-        lax.fori_loop(1, NDP, one, 0)
         pltpu.make_async_copy(sb.at[n, d], rb.at[n, d], own_sem.at[n]).start()
 
     def wait_bytes(ref, sem):
@@ -218,6 +216,7 @@
 
     convert(0)
     convert(1)
+    convert(2)
 
     wait_bytes(cpl_recv.at[pl.ds(0, NT - 1)], rcv.at[1])
     v = cpl_recv[...].reshape(256, 128).astype(F32)
@@ -234,40 +233,39 @@
 
     ones = jnp.ones((CHUNK, 128), BF16)
 
-    def gather(n):
+    def gather(n, at):
         pltpu.make_async_copy(sb.at[n, d], rb.at[n, d], own_sem.at[n]).wait()
         wait_bytes(rb.at[n, pl.ds(0, NDP - 1)], rcv.at[2 + n])
         trans[...] = rb[n].reshape(1024, 128).astype(F32)
         for jp in range(8):
-            grad[:, jp * 128:(jp + 1) * 128] = trans[pl.ds(jp, 128, stride=8), :].astype(BF16)
-        rowsum[...] += dot(grad[...], ones)
-
-    def planes(n, cols, width):
-        g = grad[...]
+            cols = slice(at + jp * 128, at + (jp + 1) * 128)
+            grad[:, cols] = trans[pl.ds(jp, 128, stride=8), :].astype(BF16)
+        rowsum[...] += dot(grad[:, at:at + CHUNK], ones)
+
+    def planes(g, v):
         for q in range(2):
-            v = nib[n, q, :, :, cols].reshape(CHUNK, width)
-            yield q, 0, dot(g, v)
+            n = v(q)
+            n = n.reshape(-1, n.shape[-1])
+            yield q, 0, dot(g, n)
             for i, k in enumerate((4, 3, 2)):
                 shift = jnp.asarray(2.0 ** (7 + k), BF16)
-                yield q, i + 1, dot(g, (v + shift) - shift)
+                yield q, i + 1, dot(g, (n + shift) - shift)
 
     def accumulate(n, _):
-        gather(n)
-        for q, i, v in planes(n, pl.ds(0, WORDS), WORDS):
+        gather(n, 0)
+        for q, i, v in planes(grad[:, 0:CHUNK], lambda q: nib[n, q]):
             acc[q, i] += v
         return 0
 
-    accumulate(0, 0)
-    convert(2)
-    accumulate(1, 0)
+    lax.fori_loop(0, 2, accumulate, 0)
     convert(3)
-    accumulate(2, 0)
-    gather(3)
+    gather(2, 0)
+    gather(3, CHUNK)
 
     def compute(s):
         per, base = PER[s], BEFORE[s]
         got = {}
-        for q, i, v in planes(3, pl.ds(STARTS[s], WIDTHS[s]), WIDTHS[s]):
+        for q, i, v in planes(grad[...], lambda q: nib[2:4, q, :, :, pl.ds(STARTS[s], WIDTHS[s])]):
             got[q, i] = v
         r = rowsum[...]
         for h in range(per // 8):
@@ -382,7 +380,7 @@
             ).start()
             return 0
 
-        lax.fori_loop(1, 16, one, 0)
+        lax.fori_loop(1, 16, one, 0, unroll=True)
 
     def owned(s, score):
         per, base = PER[s], BEFORE[s]
@@ -401,7 +399,7 @@
                 total = total + feat[pl.ds(row, 1), :] * bank[:, cols].astype(F32)
             return total
 
-        score = lax.fori_loop(0, 8, one, score)
+        score = lax.fori_loop(0, 8, one, score, unroll=True)
         return score
 
     compute(0)
@@ -416,9 +414,12 @@
     along(4)
     c_bank.wait()
     c_vrows.wait()
-    for s in range(NS):
-        across(s)
     score = jnp.zeros((128, 128), F32)
+    across(0)
+    across(1)
+    across(2)
+    across(3)
+    across(4)
     for s in range(NS):
         score = owned(s, score)
 
@@ -477,7 +478,7 @@
             vmem((4, NDP, 64, 128), BF16),
             vmem((4, NDP, 64, 128), BF16),
             vmem((1024, 128), F32),
-            vmem((128, CHUNK), BF16),
+            vmem((128, 2 * CHUNK), BF16),
             vmem((2, 4, 128, WORDS), F32),
             vmem((128, 128), F32),
             vmem((128 * 64, 128), F32),

time: 52.7 us -> 51.9 us (0.985)
  Pallas kernels: 51.8 us -> 51.1 us
    pallas_call x1, Pallas kernels: 50.4 us -> 49.7 us  [per_device(): pl.pallas_call(body, out_shape=jax.ShapeDtypeStruct((72, 128), F32), in_s...]
where the time goes in v3:
time: 51.9 us; the launch traced here: 51.7 us
  Pallas kernels  51.1 us (98%)
  between operations  0.64 us (1%)
    pallas_call x1, Pallas kernels, per_device(): pl.pallas_call(body, out_shape=jax.ShapeDtypeStruct((72, 128), F32), in_s...  49.7 us
    pallas_call x1, Pallas kernels, per_device(): pl.pallas_call(split, out_shape=(jax.ShapeDtypeStruct((64, 128), F32), ja...  1.39 us

profile of v3, /device:TPU:0, one launch (start us, length us, event | category | flops | bytes accessed | tf_op | source)
XLA Modules:
  0.0 51.7 jit_solution(6511997822959796972)
XLA Ops:
  0.6 49.7 %shard_map.95.both = f32[72,128]{1,0:T(8,128)} custom-call(bf16[512,4096]{1,0:T(8,128)(2,1)} %bitcast.7, bf16[512,512]{1,0:T(8,128)(2,1)} %bitcast.8, bf16[64,4096]{1,0:T(8,128)(2,1)} %down_hbm.1, bf16[64,512]{1,0:T(8,128)(2,1)} %bitcast.9, s32[8]{0:T(128)} %counts.1, s32[32,128,1024]{2,1,0:T(8,128)} %bitcast.6, bf16[128,8192]{1,0:T(8,128)(2,1)} %bank_hbm.1, ...), custom_call_target="tpu_custom_call" | custom-call | tf_op jit(solution)/shard_map/pallas_call | solution.py:455
  50.4 1.4 %shard_map.96 = (f32[64,128]{1,0:T(8,128)}, f32[1,64]{1,0:T(1,128)}) custom-call(f32[72,128]{1,0:T(8,128)} %shard_map.95.both), custom_call_target="tpu_custom_call" | custom-call | tf_op jit(solution)/shard_map/pallas_call | solution.py:514
